TPU v7x, 128 devices: a whole 4x4x4 slice. The times are simulated.
128 devices in a mesh: dp: 4 (over x), tensor: 2 (over core), expert: 16 (over z, y).
Axes of the slice: x: 4, y: 4, z: 4, core: 2. Of those that a mesh axis runs over, the one named last changes fastest.
Arguments:
- tokens: bfloat16 [8192, 2304], P(('dp', 'tensor', 'expert')), may hold values from -6 to 6
- routes: int32 [8192, 2], P(('dp', 'tensor', 'expert')), may hold values from 0 to 7, all different within a row; in each aligned block of 64 rows (0 to 63, 64 to 127, ...) at most 24 rows name the same one
- gates: float32 [8192, 2], P(('dp', 'tensor', 'expert')), may hold values from 0.2 to 1
- segments: int32 [8192], P(('dp', 'tensor', 'expert')), may hold values from 0 to 31, never falling along the last dimension, each value on 1 to 512 neighbouring positions
- w_gate: bfloat16 [16, 2304, 3840], P('expert', None, ('dp', 'tensor')), may hold values from -0.125 to 0.125
- w_up: bfloat16 [16, 2304, 3840], P('expert', None, ('dp', 'tensor')), may hold values from -0.125 to 0.125
- w_down: bfloat16 [16, 3840, 2304], P('expert', ('dp', 'tensor')), may hold values from -0.0625 to 0.0625
Outputs:
- embedded: bfloat16 [8192, 2304], P(('dp', 'tensor', 'expert'))
- pooled: float32 [32, 2304], replicated
Inputs may be any that keep to these rules, and one draw needn't show every extreme that they name: `routes`: each residue names two different experts. Within the rows of one device no expert is named more than 24 times, and in every draw some expert is named exactly 24 times by the rows of some device. `segments`: sequence numbers never fall along the residues; each sequence has 1 to 512 residues and one has exactly 512.
All inputs are finite; a program needn't handle non-finite values.
Results may differ from a plain program's by a relative error of at most 0.0085.
Values may be sent and summed in bfloat16 or wider, within the bound.
A program may use at most 64 MiB of HBM per device.

v0:
```python
import jax
import jax.numpy as jnp
from jax import lax
from jax.sharding import PartitionSpec as P

EXPERTS = 8
TOP = 2
CAP = 24
epsilon = 1e-06


def norm_tokens(tokens):
    values = tokens.astype(jnp.float32)
    scale = lax.rsqrt(jnp.mean(values * values, axis=1, keepdims=True) + epsilon)
    return (values, (values * scale).astype(jnp.bfloat16))


def slot_numbers(routes):
    flat_routes = routes.reshape(-1)
    onehot = (flat_routes[:, None] == jnp.arange(EXPERTS, dtype=jnp.int32)[None, :]).astype(
        jnp.int32
    )
    before = jnp.cumsum(onehot, axis=0) - onehot
    slot_rank = jnp.sum(before * onehot, axis=1)
    return flat_routes * CAP + slot_rank


def placement_matrix(slot_index, tok_count):
    hits = (jnp.arange(EXPERTS * CAP, dtype=jnp.int32)[:, None] == slot_index[None, :]).astype(
        jnp.int32
    )
    return jnp.sum(hits.reshape(EXPERTS * CAP, tok_count, TOP), axis=2).astype(jnp.bfloat16)


def fan_out(slot_rows, replicas):
    leading = slot_rows.shape[:-2]
    features = slot_rows.shape[-1]
    shaped = slot_rows.reshape(leading + (EXPERTS, CAP, features))
    shaped = jnp.repeat(shaped, replicas, axis=len(leading))
    return shaped.reshape(leading + (EXPERTS * replicas * CAP, features))


def expert_hidden(row_block, w_gate, w_up):
    gate_proj = jnp.einsum("nacd,adf->nacf", row_block, w_gate, preferred_element_type=jnp.float32)
    up_proj = jnp.einsum("nacd,adf->nacf", row_block, w_up, preferred_element_type=jnp.float32)
    return (jax.nn.silu(gate_proj) * up_proj).astype(jnp.bfloat16)


def shards(tokens, routes, gates, segments, w_gate, w_up, w_down):
    tok_count = tokens.shape[0]
    width = tokens.shape[1]
    experts_axis = lax.axis_size("expert")
    per_device = w_gate.shape[0]
    replicas = max(1, experts_axis // EXPERTS)
    plane = lax.axis_size("dp") * lax.axis_size("tensor")
    values, normed = norm_tokens(tokens)
    slot_index = slot_numbers(routes)
    placing = placement_matrix(slot_index, tok_count)
    slot_rows = jnp.dot(placing, normed, preferred_element_type=jnp.float32).astype(jnp.bfloat16)
    send_rows = fan_out(slot_rows, replicas)
    received = lax.all_to_all(send_rows, "expert", split_axis=0, concat_axis=0, tiled=True)
    local_rows = received.reshape(experts_axis, per_device, CAP, width)
    hidden = expert_hidden(
        lax.all_gather(local_rows, ("dp", "tensor"), axis=0, tiled=True), w_gate, w_up
    )
    summed = lax.psum_scatter(
        jnp.einsum("nacf,afd->nacd", hidden, w_down, preferred_element_type=jnp.float32).astype(
            jnp.bfloat16
        ),
        ("dp", "tensor"),
        scatter_dimension=0,
        tiled=True,
    )
    returned = lax.all_to_all(summed, "expert", split_axis=0, concat_axis=0, tiled=True).astype(
        jnp.float32
    )
    expert_out = jnp.sum(returned.reshape(EXPERTS, replicas, CAP, width), axis=1)
    picked = jnp.take(expert_out.reshape(EXPERTS * CAP, width), slot_index, axis=0).reshape(
        tok_count, TOP, width
    )
    mixed = values + jnp.sum(gates[:, :, None] * picked, axis=1)
    embedded = mixed.astype(jnp.bfloat16)
    devices_all = plane * experts_axis
    seq_total = tok_count * devices_all // 256
    seq_hot = (jnp.arange(seq_total, dtype=jnp.int32)[:, None] == segments[None, :]).astype(
        jnp.bfloat16
    )
    seq_sums = jnp.dot(seq_hot, embedded, preferred_element_type=jnp.float32)
    seq_counts = jnp.sum(seq_hot.astype(jnp.float32), axis=1)
    total_sums, total_counts = lax.psum((seq_sums, seq_counts), ("dp", "tensor", "expert"))
    pooled = total_sums / total_counts[:, None]
    return (embedded, pooled)


def solution(mesh):
    placed = (
        P(("dp", "tensor", "expert"), None),
        P(("dp", "tensor", "expert"), None),
        P(("dp", "tensor", "expert"), None),
        P(("dp", "tensor", "expert")),
        P("expert", None, ("dp", "tensor")),
        P("expert", None, ("dp", "tensor")),
        P("expert", ("dp", "tensor"), None),
    )
    return jax.shard_map(
        shards,
        mesh=mesh,
        in_specs=placed,
        out_specs=(P(("dp", "tensor", "expert"), None), P()),
        check_vma=False,
    )
```

profile of v0, /device:TPU:1, one launch (start us, length us, event | category | flops | bytes accessed | tf_op | source)
XLA Modules:
  0.0 430.2 jit_solution(17965702247409334811)
XLA Ops:
  7.2 0.9 copy.33
  8.9 0.7 compare_and_fusion
  9.7 1.1 fusion.9
  10.9 1.4 convolution_convert_fusion
  12.4 32.4 %all_to_all.14 = bf16[16,24,2304]{2,1,0:T(8,128)(2,1)S(1)} all-to-all(bf16[16,24,2304]{2,1,0:T(8,128)(2,1)S(1)} %bitcast.63), channel_id=1, replica_groups=mesh['dp'=4,'tensor'=2,'expert'=16] {'expert'}, dimensions={0} | all-to-all | bytes 3538944 | tf_op jit(solution)/shard_map/all_to_all | solution.py:61
  44.8 1.5 copy.36
  46.4 73.1 %all-gather.3.cloned.1.call-done = bf16[128,24,2304]{2,0,1:T(8,128)(2,1)} async-done(((bf16[16,24,2304]{2,0,1:T(8,128)(2,1)}), bf16[128,24,2304]{2,0,1:T(8,128)(2,1)}) %all-gather.3.cloned.1.call-update) | async-done | bytes 14155792 | tf_op jit(solution)/shard_map/all_gather | solution.py:64
  119.5 11.4 %fusion.6 = f32[128,24,480]{0,2,1:T(8,128)S(1)} fusion(bf16[128,24,2304]{2,0,1:T(8,128)(2,1)} %all-gather.3.cloned.1.call-done, bf16[1,2304,480]{1,2,0:T(8,128)(2,1)} %param.12), kind=kOutput, calls=%fused_computation.13 | convolution fusion | flops 6794772480 | bytes 22265856 | tf_op jit(solution)/shard_map/nacd,adf->nacf/dot_general | solution.py:45
  130.9 8.1 %fusion = bf16[128,1,24,480]{0,3,2,1:T(8,128)(2,1)S(1)} fusion(f32[128,24,480]{0,2,1:T(8,128)S(1)} %fusion.6, bf16[128,24,2304]{2,0,1:T(8,128)(2,1)S(1)} %copy-done.5, bf16[1,2304,480]{1,2,0:T(8,128)(2,1)S(1)} %copy-done.6), kind=kOutput, calls=%fused_computation.3 | convolution fusion | flops 6803619840 | bytes 25214976 | tf_op jit(solution)/shard_map/nacd,adf->nacf/dot_general | solution.py:44
  139.0 10.3 %convert_bitcast_fusion = bf16[128,1,24,2304]{3,0,2,1:T(8,128)(2,1)} fusion(bf16[128,1,24,480]{0,3,2,1:T(8,128)(2,1)S(1)} %fusion, bf16[1,480,2304]{2,1,0:T(8,128)(2,1)S(1)} %copy-done), kind=kOutput, calls=%fused_computation.1 | convolution fusion | flops 6801850368 | bytes 19316736 | tf_op jit(solution)/shard_map/nacf,afd->nacd/dot_general | solution.py:67
  149.3 79.5 %reduce-scatter.2.cloned.1.call-done = bf16[16,1,24,2304]{3,0,2,1:T(8,128)(2,1)} async-done(((bf16[128,1,24,2304]{3,0,2,1:T(8,128)(2,1)}), bf16[16,1,24,2304]{3,0,2,1:T(8,128)(2,1)}) %reduce-scatter.2.cloned.1.call-update) | async-done | bytes 1769488 | tf_op jit(solution)/shard_map/reduce_scatter | solution.py:66
  228.8 3.2 copy.37
  232.0 6.9 %all-to-all-start.1 = ((bf16[16,1,24,2304]{3,2,1,0:T(8,128)(2,1)}), bf16[16,1,24,2304]{3,2,1,0:T(8,128)(2,1)}, u32[]{:S(2)}, u32[]{:S(2)}) async-start(bf16[16,1,24,2304]{3,2,1,0:T(8,128)(2,1)} %copy.37), calls=%async_computation.2 | async-start | bytes 3538944 | tf_op jit(solution)/shard_map/all_to_all | solution.py:74
  238.9 0.2 all-reduce.2.cloned.1.call-start
  239.6 23.3 %all-to-all-done.1 = bf16[16,1,24,2304]{3,2,1,0:T(8,128)(2,1)} async-done(((bf16[16,1,24,2304]{3,2,1,0:T(8,128)(2,1)}), bf16[16,1,24,2304]{3,2,1,0:T(8,128)(2,1)}, u32[]{:S(2)}, u32[]{:S(2)}) %all-to-all-start.1) | async-done | bytes 1769504 | tf_op jit(solution)/shard_map/all_to_all | solution.py:74
  262.9 3.2 convert_reduce_fusion
  266.0 4.0 gather_fusion
  270.0 2.0 gather.7
  272.0 3.2 multiply_reduce_fusion
  275.3 1.0 fusion.11
  276.3 0.9 fusion.17
  277.4 68.6 %psum.15 = f32[32]{0:T(128)S(1)} all-reduce(f32[32]{0:T(128)S(1)} %convert_reduce_fusion.2), channel_id=1, replica_groups=mesh['dp'=4,'tensor'=2,'expert'=16] {'dp','tensor','expert'}, use_global_device_ids=true, to_apply=%region_9.10 | all-reduce | flops 32 | bytes 256 | tf_op jit(solution)/shard_map/psum | solution.py:90
  346.0 75.9 %all-reduce.2.cloned.1.call-done = f32[32,2304]{1,0:T(8,128)} async-done(((f32[32,2304]{1,0:T(8,128)}), f32[32,2304]{1,0:T(8,128)}) %all-reduce.2.cloned.1.call-update) | async-done | bytes 294928 | tf_op jit(solution)/shard_map/psum | solution.py:90
  421.9 1.8 broadcast_divide_fusion
  (36 shorter events, 1.7 us)
Async XLA Ops:
  7.2 131.8 %copy-start = (bf16[1,480,2304]{2,1,0:T(8,128)(2,1)S(1)}, bf16[1,480,2304]{2,1,0:T(8,128)(2,1)}, u32[]{:S(2)}) copy-start(bf16[1,480,2304]{2,1,0:T(8,128)(2,1)} %param.13) | copy-start | bytes 6635524
  7.2 112.3 %all-gather.3.cloned.1.call-start = ((), (), s32[]{:S(2)}) async-start(), calls=%async_computation.5 | async-start | bytes 15925248 | tf_op jit(solution)/shard_map/all_gather | solution.py:64
  46.3 182.4 %reduce-scatter.2.cloned.1.call-start = ((), (), s32[]{:S(2)}) async-start(), calls=%async_computation.3 | async-start | bytes 15925248 | tf_op jit(solution)/shard_map/reduce_scatter | solution.py:66
  119.5 11.4 %copy-start.5 = (bf16[128,24,2304]{2,0,1:T(8,128)(2,1)S(1)}, bf16[128,24,2304]{2,0,1:T(8,128)(2,1)}, u32[]{:S(2)}) copy-start(bf16[128,24,2304]{2,0,1:T(8,128)(2,1)} %all-gather.3.cloned.1.call-done) | copy-start | bytes 42467332
  119.5 11.4 %copy-start.6 = (bf16[1,2304,480]{1,2,0:T(8,128)(2,1)S(1)}, bf16[1,2304,480]{1,2,0:T(8,128)(2,1)}, u32[]{:S(2)}) copy-start(bf16[1,2304,480]{1,2,0:T(8,128)(2,1)} %param.11) | copy-start | bytes 6635524
  232.0 7.1 %copy-start.2 = (s32[64,2]{0,1:T(2,128)S(1)}, s32[64,2]{0,1:T(2,128)}, u32[]{:S(2)}) copy-start(s32[64,2]{0,1:T(2,128)} %param.8) | copy-start | bytes 1540
  232.0 7.5 %copy-start.3 = (f32[64,2]{0,1:T(2,128)S(1)}, f32[64,2]{0,1:T(2,128)}, u32[]{:S(2)}) copy-start(f32[64,2]{0,1:T(2,128)} %param.9) | copy-start | bytes 1540
  232.0 30.9 %all-to-all-start.1 = ((bf16[16,1,24,2304]{3,2,1,0:T(8,128)(2,1)}), bf16[16,1,24,2304]{3,2,1,0:T(8,128)(2,1)}, u32[]{:S(2)}, u32[]{:S(2)}) async-start(bf16[16,1,24,2304]{3,2,1,0:T(8,128)(2,1)} %copy.37), calls=%async_computation.2 | async-start | bytes 3538944 | tf_op jit(solution)/shard_map/all_to_all | solution.py:74
  238.9 183.0 %all-reduce.2.cloned.1.call-start = ((), (), s32[]{:S(2)}) async-start(), calls=%async_computation.4 | async-start | bytes 589824 | tf_op jit(solution)/shard_map/psum | solution.py:90
  270.0 6.3 %copy-start.4 = (s32[64]{0:T(128)S(1)}, s32[64]{0:T(128)}, u32[]{:S(2)}) copy-start(s32[64]{0:T(128)} %param.10) | copy-start | bytes 772
  276.3 147.3 %copy-start.1 = (bf16[64,2304]{1,0:T(8,128)(2,1)}, bf16[64,2304]{1,0:T(8,128)(2,1)S(1)}, u32[]{:S(2)}) copy-start(bf16[64,2304]{1,0:T(8,128)(2,1)S(1)} %fusion.11) | copy-start | bytes 884740
Sparse Core Ops, SparseCore 0:
  46.5 72.9 all-gather.2
  149.4 79.3 reduce-scatter.1
  277.4 144.4 all-reduce.1
where the time goes:
time: 431 us; the launch traced here: 430 us
  waiting for transfers between devices  252 us (58%)
  blocking collectives  101 us (23%)
  matrix products  32 us (7%)
  between operations  13.9 us (3%)
  local copies, waits for them, and re-layouts  12.5 us (3%)
  other arithmetic  11.7 us (3%)
  starting transfers between devices  7.18 us (2%)
    reduce_scatter x1, waiting for transfers between devices, shards(): lax.psum_scatter(jnp.einsum('nacf,afd->nacd', hidden, w_down, preferred_e...  79.5 us
    psum x1, waiting for transfers between devices, shards(): lax.psum((seq_sums, seq_counts), ('dp', 'tensor', 'expert'))  75.9 us
    all_gather x1, waiting for transfers between devices, shards(): lax.all_gather(local_rows, ('dp', 'tensor'), axis=0, tiled=True)  73.1 us
    psum x1, blocking collectives, shards(): lax.psum((seq_sums, seq_counts), ('dp', 'tensor', 'expert'))  68.6 us
    all_to_all x1, blocking collectives, shards(): lax.all_to_all(send_rows, 'expert', split_axis=0, concat_axis=0, tiled=True)  32.4 us
    all_to_all x1, waiting for transfers between devices, shards(): lax.all_to_all(summed, 'expert', split_axis=0, concat_axis=0, tiled=True)  23.3 us
    dot_general x1, matrix products, expert_hidden(): jnp.einsum('nacd,adf->nacf', row_block, w_up, preferred_element_type=jnp....  11.4 us
    dot_general x1, matrix products, shards(): jnp.einsum('nacf,afd->nacd', hidden, w_down, preferred_element_type=jnp.f...  10.3 us
  transfers between devices with their start and end apart: 4, of which 4 were waited for; matrix products, arithmetic and copies ran while one was open for 0% of the time, Pallas kernels for 0%

commit v1 on v0

--- a/solution.py
+++ b/solution.py
@@ -87,7 +87,10 @@
     )
     seq_sums = jnp.dot(seq_hot, embedded, preferred_element_type=jnp.float32)
     seq_counts = jnp.sum(seq_hot.astype(jnp.float32), axis=1)
-    total_sums, total_counts = lax.psum((seq_sums, seq_counts), ("dp", "tensor", "expert"))
+    touch_stages_all = lambda local_block, row_axis, device_axis: lax.psum(
+        lax.psum(local_block, row_axis), device_axis
+    )
+    total_sums, total_counts = touch_stages_all((seq_sums, seq_counts), ("tensor", "expert"), "dp")
     pooled = total_sums / total_counts[:, None]
     return (embedded, pooled)
 

time: 431 us -> 464 us (1.077)
  waiting for transfers between devices: 252 us -> 279 us
  blocking collectives: 101 us -> 106 us
    psum x1 -> x2, waiting for transfers between devices: 75.9 us -> 103 us  [the longest x1 103 us: shards(): lax.psum(local_block, row_axis)]
    psum x1 -> x2, blocking collectives: 68.6 us -> 73.6 us  [the longest x1 65.2 us: shards(): lax.psum(local_block, row_axis)]
  transfers between devices with their start and end apart: 4 -> 5, of which waited for: 4 -> 4; matrix products, arithmetic and copies ran while one was open for 0% -> 0% of each run, Pallas kernels for 0% -> 0%
where the time goes in v1:
time: 464 us; the launch traced here: 463 us
  waiting for transfers between devices  279 us (60%)
  blocking collectives  106 us (23%)
  matrix products  32 us (7%)
  between operations  13.9 us (3%)
  local copies, waits for them, and re-layouts  12.5 us (3%)
  other arithmetic  11.7 us (3%)
  starting transfers between devices  7.22 us (2%)
    psum x1, waiting for transfers between devices, shards(): lax.psum(local_block, row_axis)  103 us
    reduce_scatter x1, waiting for transfers between devices, shards(): lax.psum_scatter(jnp.einsum('nacf,afd->nacd', hidden, w_down, preferred_e...  79.5 us
    all_gather x1, waiting for transfers between devices, shards(): lax.all_gather(local_rows, ('dp', 'tensor'), axis=0, tiled=True)  73.1 us
    psum x1, blocking collectives, shards(): lax.psum(local_block, row_axis)  65.2 us
    all_to_all x1, blocking collectives, shards(): lax.all_to_all(send_rows, 'expert', split_axis=0, concat_axis=0, tiled=True)  32.4 us
    all_to_all x1, waiting for transfers between devices, shards(): lax.all_to_all(summed, 'expert', split_axis=0, concat_axis=0, tiled=True)  23.3 us
    dot_general x1, matrix products, expert_hidden(): jnp.einsum('nacd,adf->nacf', row_block, w_up, preferred_element_type=jnp....  11.4 us
    dot_general x1, matrix products, shards(): jnp.einsum('nacf,afd->nacd', hidden, w_down, preferred_element_type=jnp.f...  10.3 us
  transfers between devices with their start and end apart: 5, of which 4 were waited for; matrix products, arithmetic and copies ran while one was open for 0% of the time, Pallas kernels for 0%

profile of v1, /device:TPU:1, one launch (start us, length us, event | category | flops | bytes accessed | tf_op | source)
XLA Modules:
  0.0 462.6 jit_solution(10304949479997304441)
XLA Ops:
  7.2 0.9 copy.33
  8.9 0.7 compare_and_fusion
  9.7 1.1 fusion.9
  10.9 1.4 convolution_convert_fusion
  12.4 32.4 %all_to_all.14 = bf16[16,24,2304]{2,1,0:T(8,128)(2,1)S(1)} all-to-all(bf16[16,24,2304]{2,1,0:T(8,128)(2,1)S(1)} %bitcast.63), channel_id=1, replica_groups=mesh['dp'=4,'tensor'=2,'expert'=16] {'expert'}, dimensions={0} | all-to-all | bytes 3538944 | tf_op jit(solution)/shard_map/all_to_all | solution.py:61
  44.8 1.5 copy.36
  46.4 73.1 %all-gather.3.cloned.1.call-done = bf16[128,24,2304]{2,0,1:T(8,128)(2,1)} async-done(((bf16[16,24,2304]{2,0,1:T(8,128)(2,1)}), bf16[128,24,2304]{2,0,1:T(8,128)(2,1)}) %all-gather.3.cloned.1.call-update) | async-done | bytes 14155792 | tf_op jit(solution)/shard_map/all_gather | solution.py:64
  119.5 11.4 %fusion.6 = f32[128,24,480]{0,2,1:T(8,128)S(1)} fusion(bf16[128,24,2304]{2,0,1:T(8,128)(2,1)} %all-gather.3.cloned.1.call-done, bf16[1,2304,480]{1,2,0:T(8,128)(2,1)} %param.12), kind=kOutput, calls=%fused_computation.13 | convolution fusion | flops 6794772480 | bytes 22265856 | tf_op jit(solution)/shard_map/nacd,adf->nacf/dot_general | solution.py:45
  130.9 8.1 %fusion = bf16[128,1,24,480]{0,3,2,1:T(8,128)(2,1)S(1)} fusion(f32[128,24,480]{0,2,1:T(8,128)S(1)} %fusion.6, bf16[128,24,2304]{2,0,1:T(8,128)(2,1)S(1)} %copy-done.5, bf16[1,2304,480]{1,2,0:T(8,128)(2,1)S(1)} %copy-done.6), kind=kOutput, calls=%fused_computation.3 | convolution fusion | flops 6803619840 | bytes 25214976 | tf_op jit(solution)/shard_map/nacd,adf->nacf/dot_general | solution.py:44
  139.0 10.3 %convert_bitcast_fusion = bf16[128,1,24,2304]{3,0,2,1:T(8,128)(2,1)} fusion(bf16[128,1,24,480]{0,3,2,1:T(8,128)(2,1)S(1)} %fusion, bf16[1,480,2304]{2,1,0:T(8,128)(2,1)S(1)} %copy-done), kind=kOutput, calls=%fused_computation.1 | convolution fusion | flops 6801850368 | bytes 19316736 | tf_op jit(solution)/shard_map/nacf,afd->nacd/dot_general | solution.py:67
  149.3 79.5 %reduce-scatter.2.cloned.1.call-done = bf16[16,1,24,2304]{3,0,2,1:T(8,128)(2,1)} async-done(((bf16[128,1,24,2304]{3,0,2,1:T(8,128)(2,1)}), bf16[16,1,24,2304]{3,0,2,1:T(8,128)(2,1)}) %reduce-scatter.2.cloned.1.call-update) | async-done | bytes 1769488 | tf_op jit(solution)/shard_map/reduce_scatter | solution.py:66
  228.8 3.2 copy.37
  232.0 6.9 %all-to-all-start.1 = ((bf16[16,1,24,2304]{3,2,1,0:T(8,128)(2,1)}), bf16[16,1,24,2304]{3,2,1,0:T(8,128)(2,1)}, u32[]{:S(2)}, u32[]{:S(2)}) async-start(bf16[16,1,24,2304]{3,2,1,0:T(8,128)(2,1)} %copy.37), calls=%async_computation.2 | async-start | bytes 3538944 | tf_op jit(solution)/shard_map/all_to_all | solution.py:74
  239.6 23.3 %all-to-all-done.1 = bf16[16,1,24,2304]{3,2,1,0:T(8,128)(2,1)} async-done(((bf16[16,1,24,2304]{3,2,1,0:T(8,128)(2,1)}), bf16[16,1,24,2304]{3,2,1,0:T(8,128)(2,1)}, u32[]{:S(2)}, u32[]{:S(2)}) %all-to-all-start.1) | async-done | bytes 1769504 | tf_op jit(solution)/shard_map/all_to_all | solution.py:74
  262.9 3.2 convert_reduce_fusion
  266.0 4.0 gather_fusion
  270.0 2.0 gather.7
  272.0 3.2 multiply_reduce_fusion
  275.3 1.0 fusion.11
  276.3 0.9 fusion.17
  277.3 103.3 %all-reduce.3.cloned.1.call-done = f32[32,2304]{1,0:T(8,128)} async-done(((f32[32,2304]{1,0:T(8,128)}), f32[32,2304]{1,0:T(8,128)}) %all-reduce.3.cloned.1.call-update) | async-done | bytes 294928 | tf_op jit(solution)/shard_map/psum | solution.py:91
  380.7 65.2 %psum.30 = f32[32]{0:T(128)S(1)} all-reduce(f32[32]{0:T(128)S(1)} %convert_reduce_fusion.2), channel_id=1, replica_groups=mesh['dp'=4,'tensor'=2,'expert'=16] {'tensor','expert'}, use_global_device_ids=true, to_apply=%region_10.11 | all-reduce | flops 32 | bytes 256 | tf_op jit(solution)/shard_map/psum | solution.py:91
  445.9 8.4 %psum.31 = f32[32]{0:T(128)S(1)} all-reduce(f32[32]{0:T(128)S(1)} %psum.30), channel_id=1, replica_groups=mesh['dp'=4,'tensor'=2,'expert'=16] {'dp'}, use_global_device_ids=true, to_apply=%region_11.12 | all-reduce | flops 32 | bytes 256 | tf_op jit(solution)/shard_map/psum | solution.py:90
  454.3 1.8 broadcast_divide_fusion
  (40 shorter events, 2.0 us)
Async XLA Ops:
  7.2 131.8 %copy-start = (bf16[1,480,2304]{2,1,0:T(8,128)(2,1)S(1)}, bf16[1,480,2304]{2,1,0:T(8,128)(2,1)}, u32[]{:S(2)}) copy-start(bf16[1,480,2304]{2,1,0:T(8,128)(2,1)} %param.13) | copy-start | bytes 6635524
  7.2 112.3 %all-gather.3.cloned.1.call-start = ((), (), s32[]{:S(2)}) async-start(), calls=%async_computation.6 | async-start | bytes 15925248 | tf_op jit(solution)/shard_map/all_gather | solution.py:64
  46.3 182.4 %reduce-scatter.2.cloned.1.call-start = ((), (), s32[]{:S(2)}) async-start(), calls=%async_computation.3 | async-start | bytes 15925248 | tf_op jit(solution)/shard_map/reduce_scatter | solution.py:66
  119.5 11.4 %copy-start.5 = (bf16[128,24,2304]{2,0,1:T(8,128)(2,1)S(1)}, bf16[128,24,2304]{2,0,1:T(8,128)(2,1)}, u32[]{:S(2)}) copy-start(bf16[128,24,2304]{2,0,1:T(8,128)(2,1)} %all-gather.3.cloned.1.call-done) | copy-start | bytes 42467332
  119.5 11.4 %copy-start.6 = (bf16[1,2304,480]{1,2,0:T(8,128)(2,1)S(1)}, bf16[1,2304,480]{1,2,0:T(8,128)(2,1)}, u32[]{:S(2)}) copy-start(bf16[1,2304,480]{1,2,0:T(8,128)(2,1)} %param.11) | copy-start | bytes 6635524
  232.0 7.1 %copy-start.2 = (s32[64,2]{0,1:T(2,128)S(1)}, s32[64,2]{0,1:T(2,128)}, u32[]{:S(2)}) copy-start(s32[64,2]{0,1:T(2,128)} %param.8) | copy-start | bytes 1540
  232.0 7.5 %copy-start.3 = (f32[64,2]{0,1:T(2,128)S(1)}, f32[64,2]{0,1:T(2,128)}, u32[]{:S(2)}) copy-start(f32[64,2]{0,1:T(2,128)} %param.9) | copy-start | bytes 1540
  232.0 30.9 %all-to-all-start.1 = ((bf16[16,1,24,2304]{3,2,1,0:T(8,128)(2,1)}), bf16[16,1,24,2304]{3,2,1,0:T(8,128)(2,1)}, u32[]{:S(2)}, u32[]{:S(2)}) async-start(bf16[16,1,24,2304]{3,2,1,0:T(8,128)(2,1)} %copy.37), calls=%async_computation.2 | async-start | bytes 3538944 | tf_op jit(solution)/shard_map/all_to_all | solution.py:74
  238.9 141.7 %all-reduce.3.cloned.1.call-start = ((), (), s32[]{:S(2)}) async-start(), calls=%async_computation.4 | async-start | bytes 589824 | tf_op jit(solution)/shard_map/psum | solution.py:91
  270.0 6.3 %copy-start.4 = (s32[64]{0:T(128)S(1)}, s32[64]{0:T(128)}, u32[]{:S(2)}) copy-start(s32[64]{0:T(128)} %param.10) | copy-start | bytes 772
  276.3 179.8 %copy-start.1 = (bf16[64,2304]{1,0:T(8,128)(2,1)}, bf16[64,2304]{1,0:T(8,128)(2,1)S(1)}, u32[]{:S(2)}) copy-start(bf16[64,2304]{1,0:T(8,128)(2,1)S(1)} %fusion.11) | copy-start | bytes 884740
  277.2 177.1 %all-reduce.5.cloned.1.call-start = ((), (), s32[]{:S(2)}) async-start(), calls=%async_computation.5 | async-start | bytes 589824 | tf_op jit(solution)/shard_map/psum | solution.py:90
Sparse Core Ops, SparseCore 0:
  46.5 72.9 all-gather.2
  149.4 79.3 reduce-scatter.1
  277.4 103.1 all-reduce.2
  382.8 39.3 all-reduce.4
